TPU v7x, 512 devices: a whole 4x4x16 slice. The times are simulated.
512 devices in a mesh: ctx: 64 (over z, x), head: 8 (over y, core).
Axes of the slice: x: 4, y: 4, z: 16, core: 2. Of those that a mesh axis runs over, the one named last changes fastest.
Arguments:
- queries: float32 [32768, 2048], P('ctx', 'head'), may hold values from -1024 to 1024
- keys: float32 [32768, 128], P('ctx'), may hold values from -1024 to 1024
- values: float32 [32768, 128], P('ctx'), may hold values from -6 to 6
- cotangent: float32 [32768, 2048], P('ctx', 'head'), may hold values from -384 to 384
- source_ids: int32 [32768], P('ctx'), may hold values from 0 to 63
- source_weights: float32 [64], replicated, may hold values from 0.25 to 4
- q_feature: float32 [16, 128, 128], P('head'), may hold values from -4 to 4
- k_feature: float32 [128, 128], replicated, may hold values from -4 to 4
Outputs:
- grad_queries: float32 [32768, 2048], P('ctx', 'head')
- grad_keys: float32 [32768, 128], P(('ctx', 'head'))
- grad_values: float32 [32768, 128], P(('ctx', 'head'))
- grad_q_feature: float32 [16, 128, 128], P('head')
- grad_k_feature: float32 [128, 128], replicated
All inputs are finite; a program needn't handle non-finite values.
Results may differ from a plain program's by a relative error of at most 0.0015.
Values sent between devices are 32-bit elements; how exact they have to be, the bound alone decides.
A program may use at most 64 MiB of HBM per device.

v0:
```python
import jax
import jax.numpy as jnp
from jax import lax
from jax.sharding import PartitionSpec as P


def entering(value, axis, join, neutral, backward):
    count, mine = (lax.axis_size(axis), lax.axis_index(axis))
    pieces = jax.tree.map(lambda part: lax.all_gather(part, axis), value)
    if backward:
        pieces = jax.tree.map(lambda part: part[::-1], pieces)
        mine = count - 1 - mine
    total = jax.tree.map(
        lambda part, zero: jnp.full_like(part, 0) + jnp.asarray(zero, part.dtype), value, neutral
    )

    def turn(position, total):
        longer = join(total, jax.tree.map(lambda part: part[position], pieces))
        return jax.tree.map(lambda new, old: jnp.where(position < mine, new, old), longer, total)

    return lax.fori_loop(0, count - 1, turn, total)


def matmul(left, right):
    return jnp.dot(left, right, precision=lax.Precision.HIGHEST, preferred_element_type=jnp.float32)


def product(form, left, right):
    return jnp.einsum(
        form, left, right, precision=lax.Precision.HIGHEST, preferred_element_type=jnp.float32
    )


def feature_map(inputs, weight):
    logits = matmul(inputs, weight)
    upper = jax.nn.softmax(logits, axis=-1)
    lower = jax.nn.softmax(-logits, axis=-1)
    return (jnp.concatenate([upper, lower], axis=-1), upper, lower)


def feature_back(inputs, weight, upper, lower, grad_feat):
    half = upper.shape[-1]
    grad_upper = grad_feat[:, :half]
    grad_lower = grad_feat[:, half:]
    grad_logits = upper * (grad_upper - jnp.sum(upper * grad_upper, axis=-1, keepdims=True))
    grad_logits = grad_logits - lower * (
        grad_lower - jnp.sum(lower * grad_lower, axis=-1, keepdims=True)
    )
    return (matmul(grad_logits, weight.T), matmul(inputs.T, grad_logits))


def causal_mask(count):
    row_index = lax.broadcasted_iota(jnp.int32, (count, count), 0)
    col_index = lax.broadcasted_iota(jnp.int32, (count, count), 1)
    return (row_index >= col_index).astype(jnp.float32)


def add_pair(earlier, later):
    return (earlier[0] + later[0], earlier[1] + later[1])


def block_terms(query_c, key_c, value_c, scaled_c, prefix, prefix_tot):
    lower_mask = causal_mask(query_c.shape[1])
    scores = product("ncf,ndf->ncd", query_c, key_c) * lower_mask
    numerator = product("ncd,nde->nce", scores, value_c) + product("ncf,nfe->nce", query_c, prefix)
    normalizer = jnp.sum(scores, axis=2) + product("ncf,nf->nc", query_c, prefix_tot)
    output = numerator / normalizer[..., None]
    grad_numer = scaled_c / normalizer[..., None]
    grad_norm = -jnp.sum(scaled_c * output, axis=2) / normalizer
    grad_scores = (product("nce,nde->ncd", grad_numer, value_c) + grad_norm[..., None]) * lower_mask
    grad_query = (
        product("ncd,ndf->ncf", grad_scores, key_c)
        + product("nce,nfe->ncf", grad_numer, prefix)
        + grad_norm[..., None] * prefix_tot[:, None, :]
    )
    grad_key = product("ncd,ncf->ndf", grad_scores, query_c)
    grad_value = product("ncd,nce->nde", scores, grad_numer)
    carried = product("ncf,nce->nfe", query_c, grad_numer)
    carried_totals = product("nc,ncf->nf", grad_norm, query_c)
    return (grad_query, grad_key, grad_value, carried, carried_totals)


def on_device(queries, keys, values, cotangent, source_ids, source_weights, q_feature, k_feature):
    head_count = q_feature.shape[0]
    width = q_feature.shape[1]
    features = 2 * q_feature.shape[2]
    rows = queries.shape[0]
    piece = min(128, rows)
    pieces = rows // piece
    source_index = lax.broadcasted_iota(jnp.int32, (1, source_weights.shape[0]), 1)
    lookup = (source_ids[:, None] == source_index).astype(jnp.float32)
    weight = jnp.sum(lookup * source_weights[None, :], axis=1)
    key_feat, key_upper, key_lower = feature_map(keys, k_feature)
    key_c = key_feat.reshape(pieces, piece, features)
    value_c = values.reshape(pieces, piece, width)
    piece_state = product("ncf,nce->nfe", key_c, value_c)
    piece_tot = jnp.sum(key_c, axis=1)
    whole_local = (jnp.sum(piece_state, axis=0), jnp.sum(piece_tot, axis=0))
    whole_zero = (jnp.zeros((features, width), jnp.float32), jnp.zeros((features,), jnp.float32))
    earlier, earlier_totals = entering(
        (whole_local[0], whole_local[1]), "ctx", add_pair, whole_zero, False
    )
    prefix = jnp.cumsum(piece_state, axis=0) - piece_state + earlier[None]
    prefix_tot = jnp.cumsum(piece_tot, axis=0) - piece_tot + earlier_totals[None]
    grad_keyfeat = jnp.zeros(key_feat.shape, jnp.float32)
    grad_vals = jnp.zeros(values.shape, jnp.float32)
    piece_carried = jnp.zeros((pieces, features, width), jnp.float32)
    piece_carried_tot = jnp.zeros((pieces, features), jnp.float32)
    query_grads = []
    weight_grads = []
    for head in range(head_count):
        query_head = queries[:, head * width : (head + 1) * width]
        query_feat, query_upper, query_lower = feature_map(query_head, q_feature[head])
        scaled = cotangent[:, head * width : (head + 1) * width] * weight[:, None]
        grad_query, grad_key, grad_value, carried, carried_totals = block_terms(
            query_feat.reshape(pieces, piece, features),
            key_c,
            value_c,
            scaled.reshape(pieces, piece, width),
            prefix,
            prefix_tot,
        )
        grad_head, grad_weight = feature_back(
            query_head,
            q_feature[head],
            query_upper,
            query_lower,
            grad_query.reshape(rows, features),
        )
        query_grads.append(grad_head)
        weight_grads.append(grad_weight)
        grad_keyfeat = grad_keyfeat + grad_key.reshape(rows, features)
        grad_vals = grad_vals + grad_value.reshape(rows, width)
        piece_carried = piece_carried + carried
        piece_carried_tot = piece_carried_tot + carried_totals
    carried_all = jnp.sum(piece_carried, axis=0)
    carried_tot = jnp.sum(piece_carried_tot, axis=0)
    inner_later = carried_all[None] - jnp.cumsum(piece_carried, axis=0)
    inner_tot = carried_tot[None] - jnp.cumsum(piece_carried_tot, axis=0)
    grad_keyfeat = grad_keyfeat + (
        product("nce,nfe->ncf", value_c, inner_later) + inner_tot[:, None, :]
    ).reshape(rows, features)
    grad_vals = grad_vals + product("ncf,nfe->nce", key_c, inner_later).reshape(rows, width)
    later, later_tot = entering((carried_all, carried_tot), "ctx", add_pair, whole_zero, True)
    grad_keyfeat = grad_keyfeat + matmul(values, later.T) + later_tot[None, :]
    grad_vals = grad_vals + matmul(key_feat, later)
    grad_key_part, grad_kweight = feature_back(keys, k_feature, key_upper, key_lower, grad_keyfeat)
    grad_keys, grad_values = (
        lax.psum_scatter(grad_key_part, "head", scatter_dimension=0, tiled=True),
        lax.psum_scatter(grad_vals, "head", scatter_dimension=0, tiled=True),
    )
    grad_qweight = lax.psum(jnp.stack(weight_grads, axis=0), "ctx")
    grad_kweight = lax.psum(grad_kweight, ("ctx", "head"))
    return (
        jnp.concatenate(query_grads, axis=1),
        grad_keys,
        grad_values,
        grad_qweight,
        grad_kweight,
    )


def solution(mesh):
    placed = (
        P("ctx", "head"),
        P("ctx", None),
        P("ctx", None),
        P("ctx", "head"),
        P("ctx"),
        P(),
        P("head", None, None),
        P(),
    )
    return jax.shard_map(
        on_device,
        mesh=mesh,
        in_specs=placed,
        out_specs=(
            P("ctx", "head"),
            P(("ctx", "head"), None),
            P(("ctx", "head"), None),
            P("head", None, None),
            P(),
        ),
        check_vma=False,
    )
```

profile of v0, /device:TPU:2, one launch (start us, length us, event | category | flops | bytes accessed | tf_op | source)
XLA Modules:
  0.0 1215.9 jit_solution(13639607046449780209)
XLA Ops:
  7.2 1.5 fusion.97
  9.8 2.1 fusion.103
  12.8 1.2 slice_multiply_fusion.1
  14.9 87.9 %all-gather.4 = f32[64,1,256]{2,1,0:T(1,128)S(1)} all-gather(f32[1,1,256]{2,1,0:T(1,128)S(1)} %bitcast.226), channel_id=3, replica_groups=mesh['ctx'=64,'head'=8] {'ctx'}, dimensions={0}, use_global_device_ids=true | all-gather | bytes 66560 | tf_op jit(solution)/shard_map/all_gather | solution.py:9
  103.5 1.3 reshape.116
  106.6 1.8 fusion.102
  108.4 1.8 fusion.104
  110.2 62.4 %all-gather.9.cloned.1.call-done = f32[16384,128]{1,0:T(8,128)} async-done(((f32[256,128]{1,0:T(8,128)}), f32[16384,128]{1,0:T(8,128)}) %all-gather.9.cloned.1.call-update) | async-done | bytes 8388624 | tf_op jit(solution)/shard_map/all_gather | solution.py:9
  172.6 106.3 %while.32 = (s32[]{:T(128)}, f32[256,128]{1,0:T(8,128)S(1)}, f32[256]{0:T(256)S(1)}, s32[]{:T(128)}, f32[64,256,128]{2,1,0:T(8,128)}, /*index=5*/f32[64,256]{1,0:T(8,128)}, s32[]{:T(128)}, s32[]{:T(128)}) while((s32[]{:T(128)}, f32[256,128]{1,0:T(8,128)S(1)}, f32[256]{0:T(256)S(1)}, s32[]{:T(128)}, f32[64,256,128]{2,1,0:T(8,128)}, ...), condition=%wide.region_15.16_spmd.clone, body=%wide.region_14.15_spmd.clone.sunk | while | flops 99076 | bytes 398459 | solution.py:21
  280.5 2.1 fusion.105
  282.9 1.3 fusion
  284.2 1.0 fusion.19
  285.3 1.6 fusion.14
  286.8 1.1 fusion.39
  287.9 1.6 fusion.15
  290.7 80.2 %all-gather.5 = f32[64,1,256]{2,1,0:T(1,128)S(1)} all-gather(f32[1,1,256]{2,1,0:T(1,128)S(1)} %bitcast.225), channel_id=5, replica_groups=mesh['ctx'=64,'head'=8] {'ctx'}, dimensions={0}, use_global_device_ids=true | all-gather | bytes 66560 | tf_op jit(solution)/shard_map/all_gather | solution.py:9
  374.8 1.8 copy.214
  376.6 1.8 copy.215
  378.4 1.4 fusion.11
  381.2 1.6 fusion.6
  385.1 1.5 fusion.44
  386.6 1.1 reduce-window_subtract_fusion
  387.7 1.5 convolution_add_fusion.2
  389.3 1.4 fusion.4
  390.7 2.0 copy.209
  392.7 1.8 copy.213
  394.5 1.0 multiply_reduce_fusion.2
  395.6 1.1 multiply_subtract_fusion.1
  396.7 1.4 convolution_bitcast_fusion.2
  398.1 1.1 multiply_reduce_fusion.4
  399.2 1.1 multiply_subtract_fusion.2
  400.3 1.3 convolution_bitcast_fusion.3
  402.3 1.7 fusion.93
  404.0 1.0 fusion.27
  405.1 1.6 fusion.7
  406.8 27.8 %all-gather.11.cloned.1.call-done = f32[16384,128]{1,0:T(8,128)} async-done(((f32[256,128]{1,0:T(8,128)}), f32[16384,128]{1,0:T(8,128)}) %all-gather.11.cloned.1.call-update) | async-done | bytes 8388624 | tf_op jit(solution)/shard_map/all_gather | solution.py:9
  434.6 7.7 rev.6
  442.2 106.4 %while.33 = (s32[]{:T(128)}, f32[256,128]{1,0:T(8,128)S(1)}, f32[256]{0:T(256)S(1)}, s32[]{:T(128)}, f32[64,256,128]{2,1,0:T(8,128)}, /*index=5*/f32[64,256]{1,0:T(8,128)}, s32[]{:T(128)}, s32[]{:T(128)}) while((s32[]{:T(128)}, f32[256,128]{1,0:T(8,128)S(1)}, f32[256]{0:T(256)S(1)}, s32[]{:T(128)}, f32[64,256,128]{2,1,0:T(8,128)}, ...), condition=%wide.region_33.34_spmd.clone, body=%wide.region_32.33_spmd.clone.sunk | while | flops 99076 | bytes 398459 | solution.py:21
  449.8 0.9 add_select_fusion.10
  454.8 0.9 add_select_fusion.10
  458.2 0.9 add_select_fusion.10
  459.9 0.9 add_select_fusion.10
  461.6 0.9 add_select_fusion.10
  465.0 0.9 add_select_fusion.10
  466.7 0.9 add_select_fusion.10
  470.0 0.9 add_select_fusion.10
  471.7 0.9 add_select_fusion.10
  473.4 0.9 add_select_fusion.10
  475.1 0.9 add_select_fusion.10
  476.8 0.9 add_select_fusion.10
  478.5 0.9 add_select_fusion.10
  483.5 0.9 add_select_fusion.10
  492.0 0.9 add_select_fusion.10
  495.4 0.9 add_select_fusion.10
  549.5 1.0 convolution_bitcast_fusion.1
  550.8 1.7 convolution_add_fusion.5
  552.6 1.3 fusion.106
  554.7 1.0 copy.180
  555.7 138.0 %all-reduce.3.cloned.1.call-done = f32[2,128,128]{1,2,0:T(8,128)} async-done(((f32[2,128,128]{1,2,0:T(8,128)}), f32[2,128,128]{1,2,0:T(8,128)}) %all-reduce.3.cloned.1.call-update) | async-done | bytes 131088 | tf_op jit(solution)/shard_map/psum | solution.py:152
  693.8 1.7 copy.181
  695.4 440.1 %all-reduce.5.cloned.1.call-done = f32[128,128]{0,1:T(8,128)} async-done(((f32[128,128]{0,1:T(8,128)}), f32[128,128]{0,1:T(8,128)}) %all-reduce.5.cloned.1.call-update) | async-done | bytes 65552 | tf_op jit(solution)/shard_map/psum | solution.py:153
  1135.6 1.6 copy.182
  1137.1 31.7 %reduce-scatter.5.cloned.1.call-done = f32[64,128]{1,0:T(8,128)} async-done(((f32[512,128]{1,0:T(8,128)}), f32[64,128]{1,0:T(8,128)}) %reduce-scatter.5.cloned.1.call-update) | async-done | bytes 32784 | tf_op jit(solution)/shard_map/reduce_scatter | solution.py:150
  1168.8 40.2 %reduce-scatter.3.cloned.1.call-done = f32[64,128]{1,0:T(8,128)} async-done(((f32[512,128]{1,0:T(8,128)}), f32[64,128]{1,0:T(8,128)}) %reduce-scatter.3.cloned.1.call-update) | async-done | bytes 32784 | tf_op jit(solution)/shard_map/reduce_scatter | solution.py:149
  (457 shorter events, 213.1 us)
Async XLA Ops:
  7.2 2.6 copy-start
  7.2 98.1 %copy-start.12 = (f32[2,128,128]{2,1,0:T(8,128)S(1)}, f32[2,128,128]{2,1,0:T(8,128)}, u32[]{:S(2)}) copy-start(f32[2,128,128]{2,1,0:T(8,128)} %param.18) | copy-start | bytes 393220
  7.2 98.1 %copy-start.4 = (f32[512,256]{1,0:T(8,128)S(1)}, f32[512,256]{1,0:T(8,128)}, u32[]{:S(2)}) copy-start(f32[512,256]{1,0:T(8,128)} %param.12) | copy-start | bytes 1572868
  7.2 165.4 %all-gather.9.cloned.1.call-start = ((), (), s32[]{:S(2)}) async-start(), calls=%async_computation.6 | async-start | bytes 8519680 | tf_op jit(solution)/shard_map/all_gather | solution.py:9
  11.9 422.7 %all-gather.11.cloned.1.call-start = ((), (), s32[]{:S(2)}) async-start(), calls=%async_computation.7 | async-start | bytes 8519680 | tf_op jit(solution)/shard_map/all_gather | solution.py:9
  105.1 174.8 %copy-start.8 = (f32[4,128,128]{1,2,0:T(8,128)S(1)}, f32[4,128,128]{1,2,0:T(8,128)}, u32[]{:S(2)}) copy-start(f32[4,128,128]{1,2,0:T(8,128)} %copy.142) | copy-start | bytes 786436
  105.3 173.6 %copy-start.10 = (f32[128,128]{0,1:T(8,128)}, f32[128,128]{0,1:T(8,128)S(1)}, u32[]{:S(2)}) copy-start(f32[128,128]{0,1:T(8,128)S(1)} %fusion.88) | copy-start | bytes 196612
  279.0 92.5 %copy-start.11 = (f32[128,128]{0,1:T(8,128)S(1)}, f32[128,128]{0,1:T(8,128)}, u32[]{:S(2)}) copy-start(f32[128,128]{0,1:T(8,128)} %copy-done.10) | copy-start | bytes 196612
  282.6 411.2 %all-reduce.3.cloned.1.call-start = ((), (), s32[]{:S(2)}) async-start(), calls=%async_computation.4 | async-start | bytes 262144 | tf_op jit(solution)/shard_map/psum | solution.py:152
  290.6 90.5 %copy-start.15 = (f32[256]{0:T(256)}, f32[256]{0:T(256)S(1)}, u32[]{:S(2)}) copy-start(f32[256]{0:T(256)S(1)} %get-tuple-element.329) | copy-start | bytes 3076
  372.0 0.7 copy-start.6
  379.8 0.7 copy-start.7
  382.8 11.8 copy-start.3
  396.6 3.7 copy-start.1
  406.7 728.8 %all-reduce.5.cloned.1.call-start = ((), (), s32[]{:S(2)}) async-start(), calls=%async_computation.5 | async-start | bytes 131072 | tf_op jit(solution)/shard_map/psum | solution.py:153
  434.6 114.1 %copy-start.5 = (f32[512,256]{0,1:T(8,128)S(1)}, f32[512,256]{0,1:T(8,128)}, u32[]{:S(2)}) copy-start(f32[512,256]{0,1:T(8,128)} %copy.209) | copy-start | bytes 1572868
  434.6 114.9 %copy-start.9 = (f32[512,128]{1,0:T(8,128)S(1)}, f32[512,128]{1,0:T(8,128)}, u32[]{:S(2)}) copy-start(f32[512,128]{1,0:T(8,128)} %param.13) | copy-start | bytes 786436
  434.6 118.0 %copy-start.14 = (f32[128,128]{1,0:T(8,128)S(1)}, f32[128,128]{1,0:T(8,128)}, u32[]{:S(2)}) copy-start(f32[128,128]{1,0:T(8,128)} %param.19) | copy-start | bytes 196612
  442.2 111.6 %copy-start.2 = (f32[512,128]{0,1:T(8,128)S(1)}, f32[512,128]{0,1:T(8,128)}, u32[]{:S(2)}) copy-start(f32[512,128]{0,1:T(8,128)} %copy-done.1) | copy-start | bytes 786436
  442.2 111.6 %copy-start.13 = (f32[2,128,128]{2,1,0:T(8,128)S(1)}, f32[2,128,128]{2,1,0:T(8,128)}, u32[]{:S(2)}) copy-start(f32[2,128,128]{2,1,0:T(8,128)} %param.18) | copy-start | bytes 393220
  550.5 618.3 %reduce-scatter.5.cloned.1.call-start = ((), (), s32[]{:S(2)}) async-start(), calls=%async_computation.3 | async-start | bytes 294912 | tf_op jit(solution)/shard_map/reduce_scatter | solution.py:150
  552.5 656.5 %reduce-scatter.3.cloned.1.call-start = ((), (), s32[]{:S(2)}) async-start(), calls=%async_computation.2 | async-start | bytes 294912 | tf_op jit(solution)/shard_map/reduce_scatter | solution.py:149
Sparse Core Ops, SparseCore 0:
  12.0 160.5 all-gather.8
  282.7 151.7 all-gather.10
  438.0 255.7 all-reduce.2
  699.7 435.8 all-reduce.4
  1139.0 29.7 reduce-scatter.4
  1172.0 36.9 reduce-scatter.2
where the time goes:
time: 1220 us
  waiting for transfers between devices  740 us (61%)
  blocking collectives  168 us (14%)
  other arithmetic  133 us (11%)
  local copies, waits for them, and re-layouts  116 us (10%)
  matrix products  40.1 us (3%)
  between operations  14.6 us (1%)
    psum x1, waiting for transfers between devices, on_device(): grad_kweight = lax.psum(grad_kweight, ('ctx', 'head'))  440 us
    all_gather x2, blocking collectives, entering(): pieces = jax.tree.map(lambda part: lax.all_gather(part, axis), value)  168 us
    psum x1, waiting for transfers between devices, on_device(): grad_qweight = lax.psum(jnp.stack(weight_grads, axis=0), 'ctx')  138 us
    select_n x252, other arithmetic, turn(): jnp.where(position < mine, new, old)  121 us
    all_gather x2, waiting for transfers between devices, entering(): pieces = jax.tree.map(lambda part: lax.all_gather(part, axis), value)  90.2 us
    dynamic_slice x126, local copies, waits for them, and re-layouts, turn(): longer = join(total, jax.tree.map(lambda part: part[position], pieces))  89 us
    reduce_scatter x1, waiting for transfers between devices, on_device(): lax.psum_scatter(grad_key_part, 'head', scatter_dimension=0, tiled=True)  40.2 us
    reduce_scatter x1, waiting for transfers between devices, on_device(): lax.psum_scatter(grad_vals, 'head', scatter_dimension=0, tiled=True)  31.7 us
  transfers between devices with their start and end apart: 6, of which 6 were waited for; matrix products, arithmetic and copies ran while one was open for 14% of the time, Pallas kernels for 0%

commit v1 on v0

--- a/solution.py
+++ b/solution.py
@@ -150,7 +150,7 @@
         lax.psum_scatter(grad_vals, "head", scatter_dimension=0, tiled=True),
     )
     grad_qweight = lax.psum(jnp.stack(weight_grads, axis=0), "ctx")
-    grad_kweight = lax.psum(grad_kweight, ("ctx", "head"))
+    grad_kweight = lax.psum(lax.psum(grad_kweight, "ctx"), "head")
     return (
         jnp.concatenate(query_grads, axis=1),
         grad_keys,

time: 1220 us -> 976 us (0.80)
  waiting for transfers between devices: 740 us -> 489 us
    psum x1, waiting for transfers between devices: 440 us -> 62.1 us  [on_device(): grad_kweight = lax.psum(lax.psum(grad_kweight, 'ctx'), 'head')]
    psum x1, waiting for transfers between devices: 138 us -> 256 us  [on_device(): grad_qweight = lax.psum(jnp.stack(weight_grads, axis=0), 'ctx')]
  transfers between devices with their start and end apart: 6 -> 6, of which waited for: 6 -> 6; matrix products, arithmetic and copies ran while one was open for 14% -> 7% of each run, Pallas kernels for 0% -> 0%
where the time goes in v1:
time: 976 us; the launch traced here: 967 us
  waiting for transfers between devices  489 us (50%)
  blocking collectives  168 us (17%)
  other arithmetic  133 us (14%)
  local copies, waits for them, and re-layouts  116 us (12%)
  matrix products  43.5 us (4%)
  between operations  14.6 us (1%)
    psum x1, waiting for transfers between devices, on_device(): grad_qweight = lax.psum(jnp.stack(weight_grads, axis=0), 'ctx')  256 us
    all_gather x2, blocking collectives, entering(): pieces = jax.tree.map(lambda part: lax.all_gather(part, axis), value)  168 us
    select_n x252, other arithmetic, turn(): jnp.where(position < mine, new, old)  121 us
    all_gather x2, waiting for transfers between devices, entering(): pieces = jax.tree.map(lambda part: lax.all_gather(part, axis), value)  91.4 us
    dynamic_slice x126, local copies, waits for them, and re-layouts, turn(): longer = join(total, jax.tree.map(lambda part: part[position], pieces))  89 us
    psum x1, waiting for transfers between devices, on_device(): grad_kweight = lax.psum(lax.psum(grad_kweight, 'ctx'), 'head')  62.1 us
    reduce_scatter x1, waiting for transfers between devices, on_device(): lax.psum_scatter(grad_key_part, 'head', scatter_dimension=0, tiled=True)  40.5 us
    reduce_scatter x1, waiting for transfers between devices, on_device(): lax.psum_scatter(grad_vals, 'head', scatter_dimension=0, tiled=True)  38.8 us
  transfers between devices with their start and end apart: 6, of which 6 were waited for; matrix products, arithmetic and copies ran while one was open for 7% of the time, Pallas kernels for 0%

profile of v1, /device:TPU:2, one launch (start us, length us, event | category | flops | bytes accessed | tf_op | source)
XLA Modules:
  0.0 967.1 jit_solution(702238555240656915)
XLA Ops:
  7.2 1.5 fusion.97
  9.8 2.1 fusion.103
  12.8 1.2 slice_multiply_fusion.1
  14.9 87.9 %all-gather.4 = f32[64,1,256]{2,1,0:T(1,128)S(1)} all-gather(f32[1,1,256]{2,1,0:T(1,128)S(1)} %bitcast.226), channel_id=3, replica_groups=mesh['ctx'=64,'head'=8] {'ctx'}, dimensions={0}, use_global_device_ids=true | all-gather | bytes 66560 | tf_op jit(solution)/shard_map/all_gather | solution.py:9
  103.5 1.3 reshape.116
  106.6 1.8 fusion.102
  108.4 1.8 fusion.104
  110.2 62.4 %all-gather.9.cloned.1.call-done = f32[16384,128]{1,0:T(8,128)} async-done(((f32[256,128]{1,0:T(8,128)}), f32[16384,128]{1,0:T(8,128)}) %all-gather.9.cloned.1.call-update) | async-done | bytes 8388624 | tf_op jit(solution)/shard_map/all_gather | solution.py:9
  172.6 106.3 %while.32 = (s32[]{:T(128)}, f32[256,128]{1,0:T(8,128)S(1)}, f32[256]{0:T(256)S(1)}, s32[]{:T(128)}, f32[64,256,128]{2,1,0:T(8,128)}, /*index=5*/f32[64,256]{1,0:T(8,128)}, s32[]{:T(128)}, s32[]{:T(128)}) while((s32[]{:T(128)}, f32[256,128]{1,0:T(8,128)S(1)}, f32[256]{0:T(256)S(1)}, s32[]{:T(128)}, f32[64,256,128]{2,1,0:T(8,128)}, ...), condition=%wide.region_15.16_spmd.clone, body=%wide.region_14.15_spmd.clone.sunk | while | flops 99076 | bytes 398459 | solution.py:21
  175.0 0.9 add_select_fusion.8
  178.4 0.9 add_select_fusion.8
  180.1 0.9 add_select_fusion.8
  183.4 0.9 add_select_fusion.8
  186.8 0.9 add_select_fusion.8
  191.9 0.9 add_select_fusion.8
  195.3 0.9 add_select_fusion.8
  198.6 0.9 add_select_fusion.8
  200.3 0.9 add_select_fusion.8
  203.7 0.9 add_select_fusion.8
  207.1 0.9 add_select_fusion.8
  210.4 0.9 add_select_fusion.8
  212.1 0.9 add_select_fusion.8
  215.5 0.9 add_select_fusion.8
  280.5 2.1 fusion.105
  283.0 1.3 fusion
  284.2 1.0 fusion.19
  285.3 1.6 fusion.14
  286.9 1.1 fusion.39
  287.9 1.6 fusion.15
  290.7 80.0 %all-gather.5 = f32[64,1,256]{2,1,0:T(1,128)S(1)} all-gather(f32[1,1,256]{2,1,0:T(1,128)S(1)} %bitcast.225), channel_id=5, replica_groups=mesh['ctx'=64,'head'=8] {'ctx'}, dimensions={0}, use_global_device_ids=true | all-gather | bytes 66560 | tf_op jit(solution)/shard_map/all_gather | solution.py:9
  374.7 1.8 copy.214
  376.5 1.8 copy.215
  378.3 1.4 fusion.11
  381.0 1.6 fusion.6
  384.9 1.5 fusion.44
  386.5 1.1 reduce-window_subtract_fusion
  387.6 1.5 convolution_add_fusion.2
  389.1 1.4 fusion.4
  390.6 2.0 copy.209
  392.6 1.8 copy.213
  394.4 1.0 multiply_reduce_fusion.2
  395.4 1.1 multiply_subtract_fusion.1
  396.5 1.4 convolution_bitcast_fusion.2
  397.9 1.1 multiply_reduce_fusion.4
  399.0 1.1 multiply_subtract_fusion.2
  400.2 1.3 convolution_bitcast_fusion.3
  402.2 2.4 fusion.93
  404.6 1.0 fusion.27
  405.6 28.9 %all-gather.11.cloned.1.call-done = f32[16384,128]{1,0:T(8,128)} async-done(((f32[256,128]{1,0:T(8,128)}), f32[16384,128]{1,0:T(8,128)}) %all-gather.11.cloned.1.call-update) | async-done | bytes 8388624 | tf_op jit(solution)/shard_map/all_gather | solution.py:9
  434.6 7.7 rev.6
  442.2 106.4 %while.33 = (s32[]{:T(128)}, f32[256,128]{1,0:T(8,128)S(1)}, f32[256]{0:T(256)S(1)}, s32[]{:T(128)}, f32[64,256,128]{2,1,0:T(8,128)}, /*index=5*/f32[64,256]{1,0:T(8,128)}, s32[]{:T(128)}, s32[]{:T(128)}) while((s32[]{:T(128)}, f32[256,128]{1,0:T(8,128)S(1)}, f32[256]{0:T(256)S(1)}, s32[]{:T(128)}, f32[64,256,128]{2,1,0:T(8,128)}, ...), condition=%wide.region_33.34_spmd.clone, body=%wide.region_32.33_spmd.clone.sunk | while | flops 99076 | bytes 398459 | solution.py:21
  549.4 1.0 convolution_bitcast_fusion.1
  550.5 1.7 fusion.7
  552.2 255.8 %all-reduce.6.cloned.1.call-done = (f32[2,128,128]{1,2,0:T(8,128)}, f32[128,128]{0,1:T(8,128)}) async-done(((f32[2,128,128]{1,2,0:T(8,128)}, f32[128,128]{0,1:T(8,128)}), (f32[2,128,128]{1,2,0:T(8,128)}, f32[128,128]{0,1:T(8,128)})) %all-reduce.6.cloned.1.call-update) | async-done | bytes 196624 | tf_op jit(solution)/shard_map/psum | solution.py:152
  808.3 1.7 convolution_add_fusion.5
  810.0 2.1 fusion.106
  812.2 1.2 fusion.82
  813.4 1.2 fusion.85
  814.7 1.0 copy.180
  815.7 1.7 copy.181
  817.4 62.1 %all-reduce.4.cloned.1.call-done = f32[128,128]{0,1:T(8,128)} async-done(((f32[128,128]{0,1:T(8,128)}), f32[128,128]{0,1:T(8,128)}) %all-reduce.4.cloned.1.call-update) | async-done | bytes 65552 | tf_op jit(solution)/shard_map/psum | solution.py:153
  879.4 1.6 copy.182
  881.0 38.8 %reduce-scatter.5.cloned.1.call-done = f32[64,128]{1,0:T(8,128)} async-done(((f32[512,128]{1,0:T(8,128)}), f32[64,128]{1,0:T(8,128)}) %reduce-scatter.5.cloned.1.call-update) | async-done | bytes 32784 | tf_op jit(solution)/shard_map/reduce_scatter | solution.py:150
  919.8 40.5 %reduce-scatter.3.cloned.1.call-done = f32[64,128]{1,0:T(8,128)} async-done(((f32[512,128]{1,0:T(8,128)}), f32[64,128]{1,0:T(8,128)}) %reduce-scatter.3.cloned.1.call-update) | async-done | bytes 32784 | tf_op jit(solution)/shard_map/reduce_scatter | solution.py:149
  (453 shorter events, 214.2 us)
Async XLA Ops:
  7.2 2.6 copy-start
  7.2 98.1 %copy-start.12 = (f32[2,128,128]{2,1,0:T(8,128)S(1)}, f32[2,128,128]{2,1,0:T(8,128)}, u32[]{:S(2)}) copy-start(f32[2,128,128]{2,1,0:T(8,128)} %param.18) | copy-start | bytes 393220
  7.2 98.1 %copy-start.4 = (f32[512,256]{1,0:T(8,128)S(1)}, f32[512,256]{1,0:T(8,128)}, u32[]{:S(2)}) copy-start(f32[512,256]{1,0:T(8,128)} %param.12) | copy-start | bytes 1572868
  7.2 165.4 %all-gather.9.cloned.1.call-start = ((), (), s32[]{:S(2)}) async-start(), calls=%async_computation.5 | async-start | bytes 8519680 | tf_op jit(solution)/shard_map/all_gather | solution.py:9
  11.9 422.7 %all-gather.11.cloned.1.call-start = ((), (), s32[]{:S(2)}) async-start(), calls=%async_computation.6 | async-start | bytes 8519680 | tf_op jit(solution)/shard_map/all_gather | solution.py:9
  105.1 174.8 %copy-start.8 = (f32[4,128,128]{1,2,0:T(8,128)S(1)}, f32[4,128,128]{1,2,0:T(8,128)}, u32[]{:S(2)}) copy-start(f32[4,128,128]{1,2,0:T(8,128)} %copy.142) | copy-start | bytes 786436
  105.3 173.6 %copy-start.10 = (f32[128,128]{0,1:T(8,128)}, f32[128,128]{0,1:T(8,128)S(1)}, u32[]{:S(2)}) copy-start(f32[128,128]{0,1:T(8,128)S(1)} %fusion.88) | copy-start | bytes 196612
  279.0 92.4 %copy-start.11 = (f32[128,128]{0,1:T(8,128)S(1)}, f32[128,128]{0,1:T(8,128)}, u32[]{:S(2)}) copy-start(f32[128,128]{0,1:T(8,128)} %copy-done.10) | copy-start | bytes 196612
  282.6 525.3 %all-reduce.6.cloned.1.call-start = ((), (), s32[]{:S(2)}) async-start(), calls=%async_computation.7 | async-start | bytes 393216 | tf_op jit(solution)/shard_map/psum | solution.py:152
  290.7 90.4 %copy-start.13 = (f32[256]{0:T(256)}, f32[256]{0:T(256)S(1)}, u32[]{:S(2)}) copy-start(f32[256]{0:T(256)S(1)} %get-tuple-element.331) | copy-start | bytes 3076
  371.8 0.7 copy-start.6
  379.6 0.7 copy-start.7
  382.6 11.7 %copy-start.3 = (f32[512,128]{0,1:T(8,128)S(1)}, f32[512,128]{0,1:T(8,128)}, u32[]{:S(2)}) copy-start(f32[512,128]{0,1:T(8,128)} %copy.214) | copy-start | bytes 786436
  396.5 3.7 copy-start.1
  434.6 114.0 %copy-start.5 = (f32[512,256]{0,1:T(8,128)S(1)}, f32[512,256]{0,1:T(8,128)}, u32[]{:S(2)}) copy-start(f32[512,256]{0,1:T(8,128)} %copy.209) | copy-start | bytes 1572868
  434.6 114.8 %copy-start.9 = (f32[512,128]{1,0:T(8,128)S(1)}, f32[512,128]{1,0:T(8,128)}, u32[]{:S(2)}) copy-start(f32[512,128]{1,0:T(8,128)} %param.13) | copy-start | bytes 786436
  442.2 369.9 %copy-start.2 = (f32[512,128]{0,1:T(8,128)S(1)}, f32[512,128]{0,1:T(8,128)}, u32[]{:S(2)}) copy-start(f32[512,128]{0,1:T(8,128)} %copy-done.1) | copy-start | bytes 786436
  550.5 329.0 %all-reduce.4.cloned.1.call-start = ((), (), s32[]{:S(2)}) async-start(), calls=%async_computation.4 | async-start | bytes 131072 | tf_op jit(solution)/shard_map/psum | solution.py:153
  808.0 111.8 %reduce-scatter.5.cloned.1.call-start = ((), (), s32[]{:S(2)}) async-start(), calls=%async_computation.3 | async-start | bytes 294912 | tf_op jit(solution)/shard_map/reduce_scatter | solution.py:150
  810.0 150.3 %reduce-scatter.3.cloned.1.call-start = ((), (), s32[]{:S(2)}) async-start(), calls=%async_computation.2 | async-start | bytes 294912 | tf_op jit(solution)/shard_map/reduce_scatter | solution.py:149
Sparse Core Ops, SparseCore 0:
  12.0 160.5 all-gather.8
  282.8 151.7 all-gather.10
  550.6 257.3 all-reduce.5
  810.2 69.1 all-reduce.3
  882.6 37.1 reduce-scatter.4
  923.3 36.9 reduce-scatter.2
